TPU v7x, 256 devices: a whole 4x4x8 slice. The times are simulated.
256 devices in a mesh: lang: 4 (over x), fsdp: 16 (over z, core), dp: 4 (over y).
Axes of the slice: x: 4, y: 4, z: 8, core: 2. Of those that a mesh axis runs over, the one named last changes fastest.
Arguments:
- tokens_in: bfloat16 [1024, 8192], P('dp'), may hold values from -6 to 6
- cotangent: bfloat16 [1024, 16384], P('dp', ('lang', 'fsdp')), may hold values from -6 to 6
- gate_base: bfloat16 [8192, 16384], P('dp', ('lang', 'fsdp')), may hold values from -0.0625 to 0.0625
- up_base: bfloat16 [8192, 16384], P('dp', ('lang', 'fsdp')), may hold values from -0.0625 to 0.0625
- lang_delta: bfloat16 [4, 16, 4, 4, 32768], P('lang', 'fsdp'), may hold values from -0.1796875 to 0.1796875
- lang_cell: int32 [4, 16, 4, 4], P('lang', 'fsdp'), may hold values from -1 to 127, as said below
- group_lang: int32 [4], P('dp'), may hold values from 0 to 3
- task_delta: bfloat16 [1024, 32768], P(('lang', 'fsdp')), may hold values from -0.1796875 to 0.1796875
- task_slab: int32 [1024, 1], P(('lang', 'fsdp')), may hold values from 0 to 15; in each aligned block of 16 rows (0 to 15, 16 to 31, ...) at most 2 rows name the same one
- task_cell: int32 [1024, 1], P(('lang', 'fsdp')), may hold values from 0 to 127
Outputs:
- grad_input: bfloat16 [1024, 8192], P('dp', ('lang', 'fsdp'))
- task_grad: float32 [1024, 32768], P(('lang', 'fsdp'))
Inputs may be any that keep to these rules, and one draw needn't show every extreme that they name: `lang_cell`: -1 marks an empty slot; every other entry is a cell of the slab. In every draw the list of slab 0 is full for every language. `task_slab`: among the 16 task blocks of one device, no slab is named more than 2 times; some slab is named exactly 2 times.
All inputs are finite; a program needn't handle non-finite values.
Results may differ from a plain program's by a relative error of at most 0.0063.
Values may be sent and summed in bfloat16 or wider, within the bound.
No kernel may reach another device: no remote copies, remote signals or barrier semaphores. Data moves between devices by JAX's collectives and lax.ppermute only.
A program may use at most 128 MiB of HBM per device.

v0:
```python
import jax
import jax.numpy as jnp
from jax import lax
from jax.sharding import PartitionSpec as P

D = 8192
BLK = 128


def spread(value, axis, source):
    kept = jnp.where(lax.axis_index(axis) == source, value, 0).astype(value.dtype)
    return lax.psum(kept, axis)


def place_blocks(cell_ids, tile_vals, cell_total):
    one_hot = (cell_ids[:, None] == jnp.arange(cell_total, dtype=jnp.int32)[None, :]).astype(
        jnp.bfloat16
    )
    return lax.dot_general(
        one_hot, tile_vals, (((0,), (0,)), ((), ())), preferred_element_type=jnp.float32
    )


def on_device(
    tokens_in,
    cotangent,
    gate_base,
    up_base,
    lang_delta,
    lang_cell,
    group_lang,
    task_delta,
    task_slab,
    task_cell,
):
    tile_size = BLK * BLK
    slab_cols = gate_base.shape[1]
    slab_width = slab_cols // BLK
    row_blocks = D // BLK
    group_rows = tokens_in.shape[0]
    language = group_lang[0]
    range_index = lax.axis_index("lang")
    owner_vals, owner_cells = (
        spread(lang_delta, "lang", language),
        spread(lang_cell, "lang", language),
    )
    own_tiles = lax.dynamic_index_in_dim(owner_vals[0, 0], range_index, 0, keepdims=False)
    own_cells = lax.dynamic_index_in_dim(owner_cells[0, 0], range_index, 0, keepdims=False)
    fsdp_ways = lax.axis_size("fsdp")
    held = task_delta.shape[0]
    capacity = max(2, (held + fsdp_ways - 1) // fsdp_ways)
    target = task_slab[:, 0]
    matches = (target[:, None] == jnp.arange(fsdp_ways, dtype=jnp.int32)[None, :]).astype(jnp.int32)
    slot_of = jnp.sum(jnp.cumsum(matches, axis=0) * matches, axis=1) - 1
    send_vals = (
        jnp.zeros((fsdp_ways, capacity, 2 * tile_size), jnp.bfloat16)
        .at[target, slot_of]
        .set(task_delta)
    )
    send_cells = (
        jnp.full((fsdp_ways, capacity), -1, jnp.int32).at[target, slot_of].set(task_cell[:, 0])
    )
    got_vals, got_cells = (
        lax.all_to_all(send_vals, "fsdp", split_axis=0, concat_axis=0, tiled=True),
        lax.all_to_all(send_cells, "fsdp", split_axis=0, concat_axis=0, tiled=True),
    )
    base_gate, base_up = (
        lax.all_gather(gate_base, "dp", axis=0, tiled=True),
        lax.all_gather(up_base, "dp", axis=0, tiled=True),
    )
    slot_cells = got_cells.reshape(-1)
    all_cells = jnp.concatenate([own_cells, slot_cells])
    all_tiles = jnp.concatenate([own_tiles, got_vals.reshape(-1, 2 * tile_size)], axis=0)
    changes = place_blocks(all_cells, all_tiles, row_blocks * slab_width)
    changes = changes.reshape(row_blocks, slab_width, 2, BLK, BLK)

    def as_matrix(part_index):
        return changes[:, :, part_index].transpose(0, 2, 1, 3).reshape(D, slab_cols)

    gate_matrix = (base_gate.astype(jnp.float32) + as_matrix(0)).astype(jnp.bfloat16)
    up_matrix = (base_up.astype(jnp.float32) + as_matrix(1)).astype(jnp.bfloat16)
    gate_pre = jnp.dot(tokens_in, gate_matrix, preferred_element_type=jnp.float32)
    up_pre = jnp.dot(tokens_in, up_matrix, preferred_element_type=jnp.float32)
    sigmoid_g = jax.nn.sigmoid(gate_pre)
    upstream = cotangent.astype(jnp.float32)
    d_gate = (upstream * up_pre * sigmoid_g * (1.0 + gate_pre * (1.0 - sigmoid_g))).astype(
        jnp.bfloat16
    )
    d_up = (upstream * gate_pre * sigmoid_g).astype(jnp.bfloat16)
    contract = (((1,), (1,)), ((), ()))
    partial_g = lax.dot_general(gate_matrix, d_gate, contract, preferred_element_type=jnp.float32)
    summed = lax.psum_scatter(
        partial_g + lax.dot_general(up_matrix, d_up, contract, preferred_element_type=jnp.float32),
        ("lang", "fsdp"),
        scatter_dimension=0,
        tiled=True,
    )
    grad_input = summed.T.astype(jnp.bfloat16)
    filled = slot_cells >= 0
    clamped = jnp.where(filled, slot_cells, 0)
    x_tiles = tokens_in.reshape(group_rows, row_blocks, BLK)[:, clamped // slab_width, :]
    g_tiles = d_gate.reshape(group_rows, slab_width, BLK)[:, clamped % slab_width, :]
    u_tiles = d_up.reshape(group_rows, slab_width, BLK)[:, clamped % slab_width, :]
    gate_grad = jnp.einsum("tmi,tmj->mij", x_tiles, g_tiles, preferred_element_type=jnp.float32)
    up_grad = jnp.einsum("tmi,tmj->mij", x_tiles, u_tiles, preferred_element_type=jnp.float32)
    slot_grads = jnp.concatenate(
        [gate_grad.reshape(-1, tile_size), up_grad.reshape(-1, tile_size)], axis=1
    )
    slot_grads = jnp.where(filled[:, None], slot_grads, 0.0).reshape(
        fsdp_ways, capacity, 2 * tile_size
    )
    slot_grads = lax.psum(slot_grads, "dp")
    returned = lax.all_to_all(slot_grads, "fsdp", split_axis=0, concat_axis=0, tiled=True)
    task_grad = returned[target, slot_of]
    return (grad_input, task_grad)


def solution(mesh):
    return jax.shard_map(
        on_device,
        mesh=mesh,
        in_specs=(
            P("dp", None),
            P("dp", ("lang", "fsdp")),
            P("dp", ("lang", "fsdp")),
            P("dp", ("lang", "fsdp")),
            P("lang", "fsdp", None, None, None),
            P("lang", "fsdp", None, None),
            P("dp"),
            P(("lang", "fsdp"), None),
            P(("lang", "fsdp"), None),
            P(("lang", "fsdp"), None),
        ),
        out_specs=(P("dp", ("lang", "fsdp")), P(("lang", "fsdp"), None)),
        check_vma=False,
    )
```

profile of v0, /device:TPU:9, one launch (start us, length us, event | category | flops | bytes accessed | tf_op | source)
XLA Modules:
  0.0 436.3 jit_solution(2967037532233484744)
XLA Ops:
  13.1 9.2 %all-to-all-start = ((s32[16,1,2]{2,1,0:T(1,128)}), s32[16,1,2]{2,1,0:T(1,128)S(1)}, u32[]{:S(2)}, u32[]{:S(2)}) async-start(s32[16,1,2]{2,1,0:T(1,128)} %copy.56), calls=%async_computation | async-start | bytes 16384 | tf_op jit(solution)/shard_map/all_to_all | solution.py:65
  23.0 7.4 %psum.21 = s32[1,1,4,4]{3,2,1,0:T(4,128)S(1)} all-reduce(s32[1,1,4,4]{3,2,1,0:T(4,128)S(1)} %broadcast_select_fusion.1), channel_id=1, replica_groups=mesh['lang'=4,'fsdp'=16,'dp'=4] {'lang'}, use_global_device_ids=true, to_apply=%region_0.1 | all-reduce | flops 16 | bytes 128 | tf_op jit(solution)/shard_map/psum | solution.py:12
  30.4 6.5 %copy.62 = bf16[256,8192]{0,1:T(8,128)(2,1)} copy(bf16[256,8192]{1,0:T(8,128)(2,1)} %param.10) | data formatting | bytes 8388608 | tf_op args[0]
  36.9 6.5 %copy.63 = bf16[256,64,128]{2,0,1:T(8,128)(2,1)} copy(bf16[256,64,128]{0,2,1:T(8,128)(2,1)} %bitcast.101) | data formatting | bytes 8388608 | tf_op jit(solution)/shard_map/reshape | solution.py:101
  46.3 20.2 %scatter_fusion.1 = bf16[16,2,32768]{2,1,0:T(2,128)(2,1)} fusion(bf16[16,2,32768]{2,1,0:T(2,128)(2,1)} %broadcast_in_dim.44, s32[16]{0:T(128)S(1)} %get-tuple-element.14, bf16[16,32768]{1,0:T(8,128)(2,1)S(1)} %copy-done.4), kind=kCustom, calls=%fused_computation.5 | custom fusion | bytes 3145856 | tf_op jit(solution)/shard_map/scatter | solution.py:58
  66.5 8.8 %all-to-all-start.1 = ((bf16[16,2,32768]{2,1,0:T(2,128)(2,1)}), bf16[16,2,32768]{2,1,0:T(2,128)(2,1)S(1)}, u32[]{:S(2)}, u32[]{:S(2)}) async-start(bf16[16,2,32768]{2,1,0:T(2,128)(2,1)} %scatter_fusion.1), calls=%async_computation.1 | async-start | bytes 4194304 | tf_op jit(solution)/shard_map/all_to_all | solution.py:64
  77.3 4.3 gather_fusion
  82.7 41.6 %all-to-all-done.1 = bf16[16,2,32768]{2,1,0:T(2,128)(2,1)S(1)} async-done(((bf16[16,2,32768]{2,1,0:T(2,128)(2,1)}), bf16[16,2,32768]{2,1,0:T(2,128)(2,1)S(1)}, u32[]{:S(2)}, u32[]{:S(2)}) %all-to-all-start.1) | async-done | bytes 2097184 | tf_op jit(solution)/shard_map/all_to_all | solution.py:64
  126.5 4.0 convolution_bitcast_fusion
  130.6 5.2 %copy.71 = f32[16,8,256,128]{3,2,1,0:T(8,128)S(1)} copy(f32[16,8,256,128]{3,1,2,0:T(8,128)S(1)} %convolution_bitcast_fusion) | data formatting | bytes 33554432
  135.8 6.3 %slice_bitcast_fusion = (f32[64,128,2,128]{3,1,2,0:T(8,128)}, f32[64,128,2,128]{3,1,2,0:T(8,128)}) fusion(f32[64,2,2,128,128]{4,3,2,1,0:T(8,128)S(1)} %bitcast.100), kind=kLoop, calls=%fused_computation.12 | loop fusion | bytes 33554432 | tf_op jit(solution)/shard_map/transpose | solution.py:78
  142.1 15.5 %copy.57 = f32[64,128,2,128]{3,2,1,0:T(2,128)} copy(f32[64,128,2,128]{3,1,2,0:T(8,128)} %get-tuple-element.17) | data formatting | bytes 16777216 | tf_op jit(solution)/shard_map/transpose | solution.py:78
  157.6 7.8 %copy.59 = f32[64,128,2,128]{3,2,1,0:T(2,128)} copy(f32[64,128,2,128]{3,1,2,0:T(8,128)S(1)} %copy-done) | data formatting | bytes 16777216 | tf_op jit(solution)/shard_map/transpose | solution.py:78
  165.4 7.8 %fusion.16 = (bf16[256,256]{0,1:T(8,128)(2,1)S(1)}, f32[256,256]{0,1:T(8,128)S(1)}) fusion(bf16[256,256]{0,1:T(8,128)(2,1)S(1)} %copy.58, bf16[256,8192]{1,0:T(8,128)(2,1)} %param.10, f32[1024,8,2,128]{3,2,1,0:T(2,128)} %bitcast.96, bf16[8192,256]{1,0:T(8,128)(2,1)} %all-gather.3.cloned.1.call-done), kind=kOutput, calls=%fused_computation.33 | convolution fusion | flops 1080492032 | bytes 17301504 | tf_op jit(solution)/shard_map/dot_general | solution.py:82
  175.5 3.7 fusion.5
  182.6 7.8 %fusion.14 = bf16[256,256]{0,1:T(8,128)(2,1)S(1)} fusion(bf16[256,8192]{1,0:T(8,128)(2,1)} %param.10, bf16[256,256]{0,1:T(8,128)(2,1)S(1)} %copy.58, f32[256,256]{0,1:T(8,128)S(1)} %get-tuple-element.19, f32[1024,8,2,128]{3,2,1,0:T(2,128)} %bitcast.98, bf16[8192,256]{1,0:T(8,128)(2,1)} %all-gather.5.cloned.1.call-done), kind=kOutput, calls=%fused_computation.29 | convolution fusion | flops 1080754176 | bytes 17301504 | tf_op jit(solution)/shard_map/dot_general | solution.py:83
  192.7 3.7 fusion.7
  196.4 3.7 concatenate.22
  200.1 6.0 %maximum_select_fusion = f32[16,2,32768]{2,1,0:T(2,128)} fusion(f32[16,2,16384]{2,1,0:T(2,128)S(1)} %copy-done.3, f32[16,2,16384]{2,1,0:T(2,128)} %concatenate.22, pred[16,2]{1,0:T(8,128)(4,1)S(1)} %copy.61), kind=kLoop, calls=%fused_computation.14 | loop fusion | flops 2097152 | bytes 8388640 | tf_op jit(solution)/shard_map/jit(_where)/select_n | solution.py:109
  206.2 6.0 %fusion.24 = f32[8192,256]{1,0:T(8,128)S(1)} fusion(bf16[256,256]{0,1:T(8,128)(2,1)S(1)} %fusion.14, f32[1024,8,2,128]{3,2,1,0:T(2,128)} %bitcast.97, bf16[8192,256]{1,0:T(8,128)(2,1)} %all-gather.3.cloned.1.call-done), kind=kOutput, calls=%fused_computation.66 | convolution fusion | flops 1080033280 | bytes 21102592 | tf_op jit(solution)/shard_map/dot_general | solution.py:91
  212.2 8.9 %convolution_add_fusion = f32[8192,256]{1,0:T(8,128)} fusion(f32[8192,256]{1,0:T(8,128)S(1)} %fusion.24, bf16[256,256]{0,1:T(8,128)(2,1)S(1)} %get-tuple-element.18, f32[1024,8,2,128]{3,2,1,0:T(2,128)} %bitcast.99, bf16[8192,256]{1,0:T(8,128)(2,1)S(1)} %copy-done.2), kind=kOutput, calls=%fused_computation.6 | convolution fusion | flops 1082130432 | bytes 29491200 | tf_op jit(solution)/shard_map/dot_general | solution.py:93
  221.1 79.1 %all-reduce.5.cloned.1.call-done = f32[16,2,32768]{2,1,0:T(2,128)} async-done(((f32[16,2,32768]{2,1,0:T(2,128)}), f32[16,2,32768]{2,1,0:T(2,128)}) %all-reduce.5.cloned.1.call-update) | async-done | bytes 4194320 | tf_op jit(solution)/shard_map/psum | solution.py:112
  300.1 122.0 %all_to_all.19 = f32[16,2,32768]{2,1,0:T(2,128)} all-to-all(f32[16,2,32768]{2,1,0:T(2,128)} %all-reduce.5.cloned.1.call-done), channel_id=1, replica_groups=mesh['lang'=4,'fsdp'=16,'dp'=4] {'fsdp'}, dimensions={0} | all-to-all | bytes 8388608 | tf_op jit(solution)/shard_map/all_to_all | solution.py:113
  422.1 4.9 %gather_fusion.3 = f32[16,32768]{1,0:T(8,128)} fusion(f32[16,2,32768]{2,1,0:T(2,128)} %all_to_all.19, s32[16]{0:T(128)S(1)} %bitcast.104), kind=kCustom, calls=%fused_computation.3 | custom fusion | bytes 4194432 | tf_op jit(solution)/shard_map/gather | solution.py:114
  (66 shorter events, 22.8 us)
Async XLA Ops:
  8.0 2.8 copy-start.6
  8.0 3.1 copy-start.8
  8.0 14.8 %copy-start.5 = (bf16[256,256]{1,0:T(8,128)(2,1)S(1)}, bf16[256,256]{1,0:T(8,128)(2,1)}, u32[]{:S(2)}) copy-start(bf16[256,256]{1,0:T(8,128)(2,1)} %param.11) | copy-start | bytes 393220
  8.0 14.9 %copy-start.7 = (s32[1,1,4,4]{3,2,1,0:T(4,128)S(1)}, s32[1,1,4,4]{3,2,1,0:T(4,128)}, u32[]{:S(2)}) copy-start(s32[1,1,4,4]{3,2,1,0:T(4,128)} %param.15) | copy-start | bytes 196
  8.0 73.6 %all-reduce.3.cloned.1.call-start = ((), (), s32[]{:S(2)}) async-start(), calls=%async_computation.5 | async-start | bytes 2097152 | tf_op jit(solution)/shard_map/psum | solution.py:12
  10.2 155.2 %all-gather.3.cloned.1.call-start = ((), (), s32[]{:S(2)}) async-start(), calls=%async_computation.4 | async-start | bytes 5242880 | tf_op jit(solution)/shard_map/all_gather | solution.py:68
  13.1 53.5 %all-to-all-start = ((s32[16,1,2]{2,1,0:T(1,128)}), s32[16,1,2]{2,1,0:T(1,128)S(1)}, u32[]{:S(2)}, u32[]{:S(2)}) async-start(s32[16,1,2]{2,1,0:T(1,128)} %copy.56), calls=%async_computation | async-start | bytes 16384 | tf_op jit(solution)/shard_map/all_to_all | solution.py:65
  22.2 160.4 %all-gather.5.cloned.1.call-start = ((), (), s32[]{:S(2)}) async-start(), calls=%async_computation.6 | async-start | bytes 5242880 | tf_op jit(solution)/shard_map/all_gather | solution.py:69
  36.9 9.4 %copy-start.4 = (bf16[16,32768]{1,0:T(8,128)(2,1)S(1)}, bf16[16,32768]{1,0:T(8,128)(2,1)}, u32[]{:S(2)}) copy-start(bf16[16,32768]{1,0:T(8,128)(2,1)} %param.17) | copy-start | bytes 3145732
  66.5 57.8 %all-to-all-start.1 = ((bf16[16,2,32768]{2,1,0:T(2,128)(2,1)}), bf16[16,2,32768]{2,1,0:T(2,128)(2,1)S(1)}, u32[]{:S(2)}, u32[]{:S(2)}) async-start(bf16[16,2,32768]{2,1,0:T(2,128)(2,1)} %scatter_fusion.1), calls=%async_computation.1 | async-start | bytes 4194304 | tf_op jit(solution)/shard_map/all_to_all | solution.py:64
  75.4 224.8 %all-reduce.5.cloned.1.call-start = ((), (), s32[]{:S(2)}) async-start(), calls=%async_computation.8 | async-start | bytes 8388608 | tf_op jit(solution)/shard_map/psum | solution.py:112
  142.1 15.5 %copy-start = (f32[64,128,2,128]{3,1,2,0:T(8,128)S(1)}, f32[64,128,2,128]{3,1,2,0:T(8,128)}, u32[]{:S(2)}) copy-start(f32[64,128,2,128]{3,1,2,0:T(8,128)} %get-tuple-element.16) | copy-start | bytes 25165828
  173.2 2.3 copy-start.1
  196.4 3.7 copy-start.3
  206.1 220.9 %reduce-scatter.2.cloned.1.call-start = ((), (), s32[]{:S(2)}) async-start(), calls=%async_computation.7 | async-start | bytes 8519680 | tf_op jit(solution)/shard_map/reduce_scatter | solution.py:92
  206.2 6.0 %copy-start.2 = (bf16[8192,256]{1,0:T(8,128)(2,1)S(1)}, bf16[8192,256]{1,0:T(8,128)(2,1)}, u32[]{:S(2)}) copy-start(bf16[8192,256]{1,0:T(8,128)(2,1)} %all-gather.5.cloned.1.call-done) | copy-start | bytes 12582916
Sparse Core Ops, SparseCore 0:
  11.2 52.1 all-reduce.2
  221.2 187.6 reduce-scatter.1
Sparse Core Ops, SparseCore 1:
  12.6 53.6 all-gather.2
  68.0 51.0 all-gather.4
  206.2 93.9 all-reduce.4
where the time goes:
time: 437 us; the launch traced here: 436 us
  blocking collectives  129 us (30%)
  waiting for transfers between devices  122 us (28%)
  local copies, waits for them, and re-layouts  98.8 us (23%)
  matrix products  41.9 us (10%)
  starting transfers between devices  18.4 us (4%)
  between operations  16.6 us (4%)
  other arithmetic  9.44 us (2%)
    all_to_all x1, blocking collectives, on_device(): lax.all_to_all(slot_grads, 'fsdp', split_axis=0, concat_axis=0, tiled=True)  122 us
    psum x1, waiting for transfers between devices, on_device(): slot_grads = lax.psum(slot_grads, 'dp')  79.1 us
    all_to_all x1, waiting for transfers between devices, on_device(): lax.all_to_all(send_vals, 'fsdp', split_axis=0, concat_axis=0, tiled=True)  41.6 us
    transpose x3, local copies, waits for them, and re-layouts, as_matrix(): return changes[:, :, part_index].transpose(0, 2, 1, 3).reshape(D, slab_cols)  29.6 us
    scatter x1, local copies, waits for them, and re-layouts, on_device(): send_vals = jnp.zeros((fsdp_ways, capacity, 2 * tile_size), jnp.bfloat16)...  20.2 us
    unnamed x22, local copies, waits for them, and re-layouts  12.6 us
    all_to_all x1, starting transfers between devices, on_device(): lax.all_to_all(send_cells, 'fsdp', split_axis=0, concat_axis=0, tiled=True)  9.15 us
    dot_general x1, matrix products, on_device(): lax.dot_general(up_matrix, d_up, contract, preferred_element_type=jnp.flo...  8.88 us
  transfers between devices with their start and end apart: 7, of which 2 were waited for; matrix products, arithmetic and copies ran while one was open for 28% of the time, Pallas kernels for 0%

commit v1 on v0

--- a/solution.py
+++ b/solution.py
@@ -109,7 +109,7 @@
     slot_grads = jnp.where(filled[:, None], slot_grads, 0.0).reshape(
         fsdp_ways, capacity, 2 * tile_size
     )
-    slot_grads = lax.psum(slot_grads, "dp")
+    slot_grads = jnp.sum(lax.all_gather(slot_grads, "dp"), axis=0)
     returned = lax.all_to_all(slot_grads, "fsdp", split_axis=0, concat_axis=0, tiled=True)
     task_grad = returned[target, slot_of]
     return (grad_input, task_grad)

time: 437 us -> 501 us (1.15); the launches traced: 436 us -> 492 us
  waiting for transfers between devices: 122 us -> 273 us
  blocking collectives: 129 us -> 7.42 us
  local copies, waits for them, and re-layouts: 98.8 us -> 111 us
  starting transfers between devices: 18.4 us -> 26.7 us
  other arithmetic: 9.44 us -> 15.1 us
    all_gather x0 -> x1, waiting for transfers between devices: none -> 138 us  [on_device(): slot_grads = jnp.sum(lax.all_gather(slot_grads, 'dp'), axis=0)]
    all_to_all x1 -> x0, blocking collectives: 122 us -> none  [on_device(): lax.all_to_all(slot_grads, 'fsdp', split_axis=0, concat_axis=0, tiled=True)]
    all_to_all x0 -> x1, waiting for transfers between devices: none -> 91.9 us  [on_device(): lax.all_to_all(slot_grads, 'fsdp', split_axis=0, concat_axis=0, tiled=True)]
    psum x1 -> x0, waiting for transfers between devices: 79.1 us -> none  [on_device(): slot_grads = lax.psum(slot_grads, 'dp')]
    reduce_sum x0 -> x1, other arithmetic: none -> 9.4 us  [on_device(): slot_grads = jnp.sum(lax.all_gather(slot_grads, 'dp'), axis=0)]
    all_to_all x0 -> x1, starting transfers between devices: none -> 7.79 us  [on_device(): lax.all_to_all(slot_grads, 'fsdp', split_axis=0, concat_axis=0, tiled=True)]
    reduce_sum x0 -> x1, local copies, waits for them, and re-layouts: none -> 7.37 us  [on_device(): slot_grads = jnp.sum(lax.all_gather(slot_grads, 'dp'), axis=0)]
    concatenate x2 -> x4, local copies, waits for them, and re-layouts: 7.14 us -> 11.5 us  [on_device(): jnp.concatenate([gate_grad.reshape(-1, tile_size), up_grad.reshape(-1, ti...]
  transfers between devices with their start and end apart: 7 -> 8, of which waited for: 2 -> 3; matrix products, arithmetic and copies ran while one was open for 28% -> 29% of each run, Pallas kernels for 0% -> 0%
where the time goes in v1:
time: 501 us; the launch traced here: 492 us
  waiting for transfers between devices  273 us (54%)
  local copies, waits for them, and re-layouts  111 us (22%)
  matrix products  42.5 us (8%)
  starting transfers between devices  26.7 us (5%)
  between operations  16.8 us (3%)
  other arithmetic  15.1 us (3%)
  blocking collectives  7.42 us (1%)
    all_gather x1, waiting for transfers between devices, on_device(): slot_grads = jnp.sum(lax.all_gather(slot_grads, 'dp'), axis=0)  138 us
    all_to_all x1, waiting for transfers between devices, on_device(): lax.all_to_all(slot_grads, 'fsdp', split_axis=0, concat_axis=0, tiled=True)  91.9 us
    all_to_all x1, waiting for transfers between devices, on_device(): lax.all_to_all(send_vals, 'fsdp', split_axis=0, concat_axis=0, tiled=True)  41.4 us
    transpose x3, local copies, waits for them, and re-layouts, as_matrix(): return changes[:, :, part_index].transpose(0, 2, 1, 3).reshape(D, slab_cols)  29.5 us
    scatter x1, local copies, waits for them, and re-layouts, on_device(): send_vals = jnp.zeros((fsdp_ways, capacity, 2 * tile_size), jnp.bfloat16)...  20.2 us
    unnamed x22, local copies, waits for them, and re-layouts  12.9 us
    concatenate x4, local copies, waits for them, and re-layouts, on_device(): jnp.concatenate([gate_grad.reshape(-1, tile_size), up_grad.reshape(-1, ti...  11.5 us
  transfers between devices with their start and end apart: 8, of which 3 were waited for; matrix products, arithmetic and copies ran while one was open for 29% of the time, Pallas kernels for 0%

profile of v1, /device:TPU:9, one launch (start us, length us, event | category | flops | bytes accessed | tf_op | source)
XLA Modules:
  0.0 491.8 jit_solution(16722234347512528749)
XLA Ops:
  13.1 9.2 %all-to-all-start = ((s32[16,1,2]{2,1,0:T(1,128)}), s32[16,1,2]{2,1,0:T(1,128)S(1)}, u32[]{:S(2)}, u32[]{:S(2)}) async-start(s32[16,1,2]{2,1,0:T(1,128)} %copy.72), calls=%async_computation | async-start | bytes 16384 | tf_op jit(solution)/shard_map/all_to_all | solution.py:65
  23.0 7.4 %psum.14 = s32[1,1,4,4]{3,2,1,0:T(4,128)S(1)} all-reduce(s32[1,1,4,4]{3,2,1,0:T(4,128)S(1)} %broadcast_select_fusion.1), channel_id=1, replica_groups=mesh['lang'=4,'fsdp'=16,'dp'=4] {'lang'}, use_global_device_ids=true, to_apply=%region_0.1 | all-reduce | flops 16 | bytes 128 | tf_op jit(solution)/shard_map/psum | solution.py:12
  30.4 6.5 %copy.77 = bf16[256,8192]{0,1:T(8,128)(2,1)} copy(bf16[256,8192]{1,0:T(8,128)(2,1)} %param.10) | data formatting | bytes 8388608 | tf_op args[0]
  36.9 6.5 %copy.78 = bf16[256,64,128]{2,0,1:T(8,128)(2,1)} copy(bf16[256,64,128]{0,2,1:T(8,128)(2,1)} %bitcast.101) | data formatting | bytes 8388608 | tf_op jit(solution)/shard_map/reshape | solution.py:101
  46.3 20.2 %scatter_fusion.1 = bf16[16,2,32768]{2,1,0:T(2,128)(2,1)} fusion(bf16[16,2,32768]{2,1,0:T(2,128)(2,1)} %broadcast_in_dim.44, s32[16]{0:T(128)S(1)} %get-tuple-element.16, bf16[16,32768]{1,0:T(8,128)(2,1)S(1)} %copy-done.4), kind=kCustom, calls=%fused_computation.5 | custom fusion | bytes 3145856 | tf_op jit(solution)/shard_map/scatter | solution.py:58
  66.5 8.8 %all-to-all-start.1 = ((bf16[16,2,32768]{2,1,0:T(2,128)(2,1)}), bf16[16,2,32768]{2,1,0:T(2,128)(2,1)S(1)}, u32[]{:S(2)}, u32[]{:S(2)}) async-start(bf16[16,2,32768]{2,1,0:T(2,128)(2,1)} %scatter_fusion.1), calls=%async_computation.1 | async-start | bytes 4194304 | tf_op jit(solution)/shard_map/all_to_all | solution.py:64
  77.4 4.4 gather_fusion
  82.9 41.4 %all-to-all-done.1 = bf16[16,2,32768]{2,1,0:T(2,128)(2,1)S(1)} async-done(((bf16[16,2,32768]{2,1,0:T(2,128)(2,1)}), bf16[16,2,32768]{2,1,0:T(2,128)(2,1)S(1)}, u32[]{:S(2)}, u32[]{:S(2)}) %all-to-all-start.1) | async-done | bytes 2097184 | tf_op jit(solution)/shard_map/all_to_all | solution.py:64
  126.5 4.0 convolution_bitcast_fusion
  130.6 5.2 %copy.89 = f32[16,8,256,128]{3,2,1,0:T(8,128)S(1)} copy(f32[16,8,256,128]{3,1,2,0:T(8,128)S(1)} %convolution_bitcast_fusion) | data formatting | bytes 33554432
  135.8 6.3 %slice_bitcast_fusion = (f32[64,128,2,128]{3,1,2,0:T(8,128)}, f32[64,128,2,128]{3,1,2,0:T(8,128)}) fusion(f32[64,2,2,128,128]{4,3,2,1,0:T(8,128)S(1)} %bitcast.100), kind=kLoop, calls=%fused_computation.12 | loop fusion | bytes 33554432 | tf_op jit(solution)/shard_map/transpose | solution.py:78
  142.1 15.5 %copy.73 = f32[64,128,2,128]{3,2,1,0:T(2,128)} copy(f32[64,128,2,128]{3,1,2,0:T(8,128)} %get-tuple-element.19) | data formatting | bytes 16777216 | tf_op jit(solution)/shard_map/transpose | solution.py:78
  157.6 7.8 %copy.75 = f32[64,128,2,128]{3,2,1,0:T(2,128)} copy(f32[64,128,2,128]{3,1,2,0:T(8,128)S(1)} %copy-done) | data formatting | bytes 16777216 | tf_op jit(solution)/shard_map/transpose | solution.py:78
  165.3 7.8 %fusion.16 = (bf16[256,256]{0,1:T(8,128)(2,1)S(1)}, f32[256,256]{0,1:T(8,128)S(1)}) fusion(bf16[256,256]{0,1:T(8,128)(2,1)S(1)} %copy.74, bf16[256,8192]{1,0:T(8,128)(2,1)} %param.10, f32[1024,8,2,128]{3,2,1,0:T(2,128)} %bitcast.96, bf16[8192,256]{1,0:T(8,128)(2,1)} %all-gather.4.cloned.1.call-done), kind=kOutput, calls=%fused_computation.33 | convolution fusion | flops 1080492032 | bytes 17301504 | tf_op jit(solution)/shard_map/dot_general | solution.py:82
  182.7 4.1 copy.84
  186.9 7.8 %fusion.14 = bf16[256,256]{0,1:T(8,128)(2,1)S(1)} fusion(bf16[256,8192]{1,0:T(8,128)(2,1)} %param.10, bf16[256,256]{0,1:T(8,128)(2,1)S(1)} %copy.74, f32[256,256]{0,1:T(8,128)S(1)} %get-tuple-element.21, f32[1024,8,2,128]{3,2,1,0:T(2,128)} %bitcast.98, bf16[8192,256]{1,0:T(8,128)(2,1)} %all-gather.6.cloned.1.call-done), kind=kOutput, calls=%fused_computation.29 | convolution fusion | flops 1080754176 | bytes 17301504 | tf_op jit(solution)/shard_map/dot_general | solution.py:83
  207.3 6.0 %fusion.24 = f32[8192,256]{1,0:T(8,128)S(1)} fusion(bf16[256,256]{0,1:T(8,128)(2,1)S(1)} %fusion.14, f32[1024,8,2,128]{3,2,1,0:T(2,128)} %bitcast.97, bf16[8192,256]{1,0:T(8,128)(2,1)} %all-gather.4.cloned.1.call-done), kind=kOutput, calls=%fused_computation.66 | convolution fusion | flops 1080033280 | bytes 21102592 | tf_op jit(solution)/shard_map/dot_general | solution.py:91
  213.3 9.5 %convolution_add_fusion = f32[8192,256]{1,0:T(8,128)} fusion(f32[8192,256]{1,0:T(8,128)S(1)} %fusion.24, bf16[256,256]{0,1:T(8,128)(2,1)S(1)} %get-tuple-element.20, f32[1024,8,2,128]{3,2,1,0:T(2,128)} %bitcast.99, bf16[8192,256]{1,0:T(8,128)(2,1)S(1)} %copy-done.2), kind=kOutput, calls=%fused_computation.6 | convolution fusion | flops 1082130432 | bytes 29491200 | tf_op jit(solution)/shard_map/dot_general | solution.py:93
  222.9 138.1 %all-gather.8.cloned.1.call-done = f32[4,16,2,32768]{3,1,2,0:T(8,128)} async-done(((f32[1,16,2,32768]{3,1,2,0:T(8,128)}), f32[4,16,2,32768]{3,1,2,0:T(8,128)}) %all-gather.8.cloned.1.call-update) | async-done | bytes 16777232 | tf_op jit(solution)/shard_map/all_gather | solution.py:112
  361.0 9.4 %reduce_sum.19 = f32[16,2,32768]{2,0,1:T(8,128)} reduce(f32[4,16,2,32768]{3,1,2,0:T(8,128)} %all-gather.8.cloned.1.call-done, f32[]{:T(128)} %constant.69.clone.1), dimensions={0}, to_apply=%region_7.8 | reduce | flops 3145728 | bytes 20971524 | tf_op jit(solution)/shard_map/reduce_sum | solution.py:112
  370.4 7.4 %copy.85 = f32[16,2,32768]{2,1,0:T(2,128)} copy(f32[16,2,32768]{2,0,1:T(8,128)} %reduce_sum.19) | data formatting | bytes 8388608 | tf_op jit(solution)/shard_map/reduce_sum | solution.py:112
  377.7 7.8 %all-to-all-start.2 = ((f32[16,2,32768]{2,1,0:T(2,128)}), f32[16,2,32768]{2,1,0:T(2,128)}, u32[]{:S(2)}, u32[]{:S(2)}) async-start(f32[16,2,32768]{2,1,0:T(2,128)} %copy.85), calls=%async_computation.3 | async-start | bytes 8388608 | tf_op jit(solution)/shard_map/all_to_all | solution.py:113
  387.2 91.9 %all-to-all-done.2 = f32[16,2,32768]{2,1,0:T(2,128)} async-done(((f32[16,2,32768]{2,1,0:T(2,128)}), f32[16,2,32768]{2,1,0:T(2,128)}, u32[]{:S(2)}, u32[]{:S(2)}) %all-to-all-start.2) | async-done | bytes 4194336 | tf_op jit(solution)/shard_map/all_to_all | solution.py:113
  479.1 4.9 gather_fusion.3
  (70 shorter events, 37.1 us)
Async XLA Ops:
  8.0 2.8 copy-start.6
  8.0 3.1 copy-start.8
  8.0 14.8 %copy-start.5 = (bf16[256,256]{1,0:T(8,128)(2,1)S(1)}, bf16[256,256]{1,0:T(8,128)(2,1)}, u32[]{:S(2)}) copy-start(bf16[256,256]{1,0:T(8,128)(2,1)} %param.11) | copy-start | bytes 393220
  8.0 14.9 %copy-start.7 = (s32[1,1,4,4]{3,2,1,0:T(4,128)S(1)}, s32[1,1,4,4]{3,2,1,0:T(4,128)}, u32[]{:S(2)}) copy-start(s32[1,1,4,4]{3,2,1,0:T(4,128)} %param.15) | copy-start | bytes 196
  8.0 73.8 %all-reduce.2.cloned.1.call-start = ((), (), s32[]{:S(2)}) async-start(), calls=%async_computation.5 | async-start | bytes 2097152 | tf_op jit(solution)/shard_map/psum | solution.py:12
  10.2 155.1 %all-gather.4.cloned.1.call-start = ((), (), s32[]{:S(2)}) async-start(), calls=%async_computation.4 | async-start | bytes 5242880 | tf_op jit(solution)/shard_map/all_gather | solution.py:68
  13.1 53.5 %all-to-all-start = ((s32[16,1,2]{2,1,0:T(1,128)}), s32[16,1,2]{2,1,0:T(1,128)S(1)}, u32[]{:S(2)}, u32[]{:S(2)}) async-start(s32[16,1,2]{2,1,0:T(1,128)} %copy.72), calls=%async_computation | async-start | bytes 16384 | tf_op jit(solution)/shard_map/all_to_all | solution.py:65
  22.2 164.6 %all-gather.6.cloned.1.call-start = ((), (), s32[]{:S(2)}) async-start(), calls=%async_computation.6 | async-start | bytes 5242880 | tf_op jit(solution)/shard_map/all_gather | solution.py:69
  36.9 9.4 %copy-start.4 = (bf16[16,32768]{1,0:T(8,128)(2,1)S(1)}, bf16[16,32768]{1,0:T(8,128)(2,1)}, u32[]{:S(2)}) copy-start(bf16[16,32768]{1,0:T(8,128)(2,1)} %param.17) | copy-start | bytes 3145732
  66.5 57.8 %all-to-all-start.1 = ((bf16[16,2,32768]{2,1,0:T(2,128)(2,1)}), bf16[16,2,32768]{2,1,0:T(2,128)(2,1)S(1)}, u32[]{:S(2)}, u32[]{:S(2)}) async-start(bf16[16,2,32768]{2,1,0:T(2,128)(2,1)} %scatter_fusion.1), calls=%async_computation.1 | async-start | bytes 4194304 | tf_op jit(solution)/shard_map/all_to_all | solution.py:64
  75.4 285.6 %all-gather.8.cloned.1.call-start = ((), (), s32[]{:S(2)}) async-start(), calls=%async_computation.8 | async-start | bytes 20971520 | tf_op jit(solution)/shard_map/all_gather | solution.py:112
  142.1 15.5 %copy-start = (f32[64,128,2,128]{3,1,2,0:T(8,128)S(1)}, f32[64,128,2,128]{3,1,2,0:T(8,128)}, u32[]{:S(2)}) copy-start(f32[64,128,2,128]{3,1,2,0:T(8,128)} %get-tuple-element.18) | copy-start | bytes 25165828
  173.1 2.3 copy-start.1
  203.2 1.6 copy-start.3
  207.1 178.5 %reduce-scatter.2.cloned.1.call-start = ((), (), s32[]{:S(2)}) async-start(), calls=%async_computation.7 | async-start | bytes 8519680 | tf_op jit(solution)/shard_map/reduce_scatter | solution.py:92
  207.3 6.0 %copy-start.2 = (bf16[8192,256]{1,0:T(8,128)(2,1)S(1)}, bf16[8192,256]{1,0:T(8,128)(2,1)}, u32[]{:S(2)}) copy-start(bf16[8192,256]{1,0:T(8,128)(2,1)} %all-gather.6.cloned.1.call-done) | copy-start | bytes 12582916
  377.7 101.4 %all-to-all-start.2 = ((f32[16,2,32768]{2,1,0:T(2,128)}), f32[16,2,32768]{2,1,0:T(2,128)}, u32[]{:S(2)}, u32[]{:S(2)}) async-start(f32[16,2,32768]{2,1,0:T(2,128)} %copy.85), calls=%async_computation.3 | async-start | bytes 8388608 | tf_op jit(solution)/shard_map/all_to_all | solution.py:113
Sparse Core Ops, SparseCore 0:
  11.2 52.1 all-reduce.1
  223.0 143.4 reduce-scatter.1
Sparse Core Ops, SparseCore 1:
  12.6 53.6 all-gather.3
  68.0 51.0 all-gather.5
  207.1 153.8 all-gather.7
